TPU v7x, 32 devices: a whole 2x2x4 slice. The times are simulated.
32 devices in a mesh: clips: 2 (over y), tm: 4 (over x, core), rows: 4 (over z).
Axes of the slice: x: 2, y: 2, z: 4, core: 2. Of those that a mesh axis runs over, the one named last changes fastest.
Arguments:
- features: bfloat16 [8, 8, 48, 384], P(('clips', 'tm'), 'rows'), parts along dimension 0, may hold values from -320 to 320
- first_gain: float32 [384], replicated, may hold values from 0.5 to 1.5
- first_shift: float32 [384], replicated, may hold values from -3 to 3
- first_kernel: bfloat16 [384, 3, 3, 3, 384], P('tm'), may hold values from -0.0625 to 0.0625
- first_bias: float32 [384], P('tm'), may hold values from -2 to 2
- second_gain: float32 [384], replicated, may hold values from 0.5 to 1.5
- second_shift: float32 [384], replicated, may hold values from -3 to 3
- second_kernel: bfloat16 [384, 3, 3, 3, 384], P('tm'), may hold values from -0.0625 to 0.0625
- second_bias: float32 [384], P('tm'), may hold values from -2 to 2
- third_gain: float32 [384], replicated, may hold values from 0.5 to 1.5
- third_shift: float32 [384], replicated, may hold values from -3 to 3
- query_weight: bfloat16 [384, 384], replicated, may hold values from -0.30618622 to 0.30618622
- key_weight: bfloat16 [384, 384], replicated, may hold values from -1.8371173 to 1.8371173
- value_weight: bfloat16 [384, 384], replicated, may hold values from -0.3125 to 0.3125
- output_weight: bfloat16 [384, 384], replicated, may hold values from -0.3125 to 0.3125
Outputs:
- decoded: bfloat16 [8, 8, 48, 384], P(('clips', 'tm'), 'rows'), parts along dimension 0
There are 2 independent parts, one for each index of `clips`. A program takes and returns all parts, laid end to end along the dimension named above; an argument that names none is the same for every part. Nothing has to cross between parts.
All inputs are finite; a program needn't handle non-finite values.
Results may differ from a plain program's by a relative error of at most 0.029.
Values may be sent and summed in bfloat16 or wider, within the bound.
A program may use at most 64 MiB of HBM per device.

v0:
```python
import jax
import jax.numpy as jnp
from jax import lax
from jax.sharding import PartitionSpec as P

C = 384
GROUPS = 32
epsilon = 1e-06


def extended(cells, sides, width):
    for axis, dim in sides:
        count = lax.axis_size(axis)
        ends = count - 1
        head = lax.slice_in_dim(cells, 0, width, axis=dim)
        tail = lax.slice_in_dim(cells, cells.shape[dim] - width, cells.shape[dim], axis=dim)
        cells = jnp.concatenate(
            [
                lax.ppermute(tail, axis, [(i, (i + 1) % count) for i in range(ends)]),
                cells,
                lax.ppermute(head, axis, [((i + 1) % count, i) for i in range(ends)]),
            ],
            axis=dim,
        )
    return cells


def group_norm(values, gain, shift):
    frame_count, row_count, col_count, channels = values.shape
    entries = lax.axis_size("rows") * row_count * col_count * (channels // GROUPS)
    grouped = values.reshape(frame_count, row_count, col_count, GROUPS, channels // GROUPS)
    sums = lax.psum(jnp.sum(grouped, axis=(1, 2, 4)), "rows")
    average = sums / entries
    centered = grouped - average[:, None, None, :, None]
    variance = lax.psum(jnp.sum(centered * centered, axis=(1, 2, 4)), "rows") / entries
    scaled = centered * lax.rsqrt(variance + epsilon)[:, None, None, :, None]
    return scaled.reshape(frame_count, row_count, col_count, channels) * gain + shift


def causal_conv(active, kernel, bias):
    widened = extended(active, (("rows", 1),), 1)
    clip_frames = lax.all_gather(widened, "tm", axis=0, tiled=True)
    frame_count, padded_rows, col_count, channels = clip_frames.shape
    row_count = padded_rows - 2
    outputs = kernel.shape[0]
    padded = jnp.pad(clip_frames, ((2, 0), (0, 0), (1, 1), (0, 0)))
    summed = jnp.zeros((outputs, frame_count * row_count * col_count), jnp.float32)
    for tap_time in range(3):
        for tap_row in range(3):
            window = padded[tap_time : tap_time + frame_count, tap_row : tap_row + row_count]
            stacked = jnp.concatenate(
                [window[:, :, shift_col : shift_col + col_count] for shift_col in range(3)], axis=-1
            )
            tap_weight = kernel[:, tap_time, tap_row].reshape(outputs, 3 * channels)
            summed = summed + lax.dot_general(
                tap_weight,
                stacked.reshape(-1, 3 * channels),
                (((1,), (1,)), ((), ())),
                preferred_element_type=jnp.float32,
            )
    result = (
        (summed + bias[:, None])
        .astype(jnp.bfloat16)
        .reshape(outputs, frame_count, row_count, col_count)
    )
    mixed = lax.all_to_all(result, "tm", split_axis=1, concat_axis=0, tiled=True)
    return jnp.transpose(mixed, (1, 2, 3, 0))


def absorb(carry, queries, keys, values):
    peak, total, summed = carry
    scores = jnp.einsum("fqc,fkc->fqk", queries, keys, preferred_element_type=jnp.float32)
    new_peak = jnp.max(scores, axis=-1)
    factor = jnp.exp(peak - new_peak)
    expon = jnp.exp(scores - new_peak[..., None])
    total = total * factor + jnp.sum(expon, axis=-1)
    summed = summed * factor[..., None] + jnp.einsum(
        "fqk,fkc->fqc", expon.astype(jnp.bfloat16), values, preferred_element_type=jnp.float32
    )
    return (new_peak, total, summed)


def per_device(
    features,
    first_gain,
    first_shift,
    first_kernel,
    first_bias,
    second_gain,
    second_shift,
    second_kernel,
    second_bias,
    third_gain,
    third_shift,
    query_weight,
    key_weight,
    value_weight,
    output_weight,
):
    frame_count, row_count, col_count, channels = features.shape
    start = features.astype(jnp.float32)
    active1 = jax.nn.silu(group_norm(start, first_gain, first_shift)).astype(jnp.bfloat16)
    conv1 = causal_conv(active1, first_kernel, first_bias)
    active2 = jax.nn.silu(group_norm(conv1.astype(jnp.float32), second_gain, second_shift)).astype(
        jnp.bfloat16
    )
    conv2 = causal_conv(active2, second_kernel, second_bias)
    hidden = (start + conv2.astype(jnp.float32)).astype(jnp.bfloat16)
    normed = group_norm(hidden.astype(jnp.float32), third_gain, third_shift).astype(jnp.bfloat16)
    flat = normed.reshape(frame_count, row_count * col_count, channels)
    queries = (
        jnp.einsum("fpc,cd->fpd", flat, query_weight, preferred_element_type=jnp.float32)
        * C ** (-0.5)
    ).astype(jnp.bfloat16)
    positions = row_count * col_count
    initial = (
        jnp.full((frame_count, positions), -jnp.inf, jnp.float32),
        jnp.zeros((frame_count, positions), jnp.float32),
        jnp.zeros((frame_count, positions, channels), jnp.float32),
    )
    keys = jnp.einsum("fpc,cd->fpd", flat, key_weight, preferred_element_type=jnp.float32).astype(
        jnp.bfloat16
    )
    values = jnp.einsum(
        "fpc,cd->fpd", flat, value_weight, preferred_element_type=jnp.float32
    ).astype(jnp.bfloat16)
    shape4 = (frame_count, row_count, col_count, channels)
    peak, total, summed = absorb(
        initial,
        queries,
        lax.all_gather(keys.reshape(shape4), "rows", axis=1, tiled=True).reshape(
            frame_count, -1, channels
        ),
        lax.all_gather(values.reshape(shape4), "rows", axis=1, tiled=True).reshape(
            frame_count, -1, channels
        ),
    )
    attended = (summed / total[..., None]).astype(jnp.bfloat16)
    projected = jnp.einsum(
        "fpc,cd->fpd", attended, output_weight, preferred_element_type=jnp.float32
    )
    decoded = hidden.astype(jnp.float32) + projected.reshape(
        frame_count, row_count, col_count, channels
    )
    return decoded.astype(jnp.bfloat16)


def solution(mesh):
    in_specs = (
        P(("clips", "tm"), "rows", None, None),
        P(),
        P(),
        P("tm", None, None, None, None),
        P("tm"),
        P(),
        P(),
        P("tm", None, None, None, None),
        P("tm"),
        P(),
        P(),
        P(),
        P(),
        P(),
        P(),
    )
    out_specs = P(("clips", "tm"), "rows", None, None)
    return jax.shard_map(
        per_device, mesh=mesh, in_specs=in_specs, out_specs=out_specs, check_vma=False
    )
```

profile of v0, /device:TPU:0, one launch (start us, length us, event | category | flops | bytes accessed | tf_op | source)
XLA Modules:
  0.0 157.3 jit_solution(10581170224222182222)
XLA Ops:
  0.0 1.0 convert_reduce_fusion.1
  1.2 13.5 %psum.42 = f32[1,32]{1,0:T(1,128)S(1)} all-reduce(f32[1,32]{1,0:T(1,128)S(1)} %bitcast.277), channel_id=1, replica_groups=mesh['clips'=2,'tm'=4,'rows'=4] {'rows'}, use_global_device_ids=true, to_apply=%region_2.0 | all-reduce | flops 32 | bytes 256 | tf_op jit(solution)/shard_map/psum | solution.py:32
  14.8 0.9 fusion.21
  16.0 8.4 %psum.43 = f32[1,32]{1,0:T(1,128)S(1)} all-reduce(f32[1,32]{1,0:T(1,128)S(1)} %bitcast.278), channel_id=1, replica_groups=mesh['clips'=2,'tm'=4,'rows'=4] {'rows'}, use_global_device_ids=true, to_apply=%region_5.6 | all-reduce | flops 32 | bytes 256 | tf_op jit(solution)/shard_map/psum | solution.py:35
  24.5 1.0 fusion.29
  25.5 3.9 %collective-permute-start = (bf16[1,1,48,384]{3,2,1,0:T(8,128)(2,1)S(1)}, bf16[1,1,48,384]{3,2,1,0:T(8,128)(2,1)S(1)}, u32[]{:S(2)}, u32[]{:S(2)}) collective-permute-start(bf16[1,1,48,384]{3,2,1,0:T(8,128)(2,1)S(1)} %get-tuple-element.81), channel_id=1, source_target_pairs={{0,1},{1,2},{2,3},{4,5},{5,6},{6,7},{8,9},{9,10},{10,11},{12,13},{... | collective-permute-start | bytes 110600 | tf_op jit(solution)/shard_map/ppermute | solution.py:19
  29.4 1.3 collective-permute-start.1
  30.7 1.8 %fusion.45 = (bf16[96,1,1,3,384]{4,0,3,2,1:T(8,128)(2,1)S(1)}, bf16[96,1,1,3,384]{4,0,3,2,1:T(8,128)(2,1)S(1)}, bf16[96,1,1,3,384]{4,0,3,2,1:T(8,128)(2,1)S(1)},...) fusion(bf16[96,3,3,3,384]{4,0,3,2,1:T(8,128)(2,1)} %param.18), kind=kLoop, calls=%fused_computation.150 | loop fusion | bytes 3981312 | tf_op jit(solution)/shard_map/slice | solution.py:54
  34.3 1.0 collective-permute-done.1
  35.3 7.5 %all_gather.12 = bf16[4,4,48,384]{3,2,1,0:T(8,128)(2,1)S(1)} all-gather(bf16[1,4,48,384]{3,2,1,0:T(8,128)(2,1)S(1)} %pad_maximum_fusion.18), channel_id=1, replica_groups=mesh['clips'=2,'tm'=4,'rows'=4] {'tm'}, dimensions={0}, use_global_device_ids=true | all-gather | bytes 737280 | tf_op jit(solution)/shard_map/all_gather | solution.py:42
  42.8 1.8 %pad_slice_fusion.25 = (bf16[4,2,48,384]{3,2,1,0:T(8,128)(2,1)S(1)}, bf16[4,2,48,384]{3,2,1,0:T(8,128)(2,1)S(1)}, bf16[4,2,48,384]{3,2,1,0:T(8,128)(2,1)S(1)}, b...) fusion(bf16[4,4,48,384]{3,2,1,0:T(8,128)(2,1)S(1)} %all_gather.12), kind=kLoop, calls=%fused_computation.25 | loop fusion | bytes 6193152 | tf_op jit(solution)/shard_map/slice | solution.py:52
  45.5 0.4 convolution_add_fusion.16
  46.1 0.4 convolution_add_fusion.15
  47.1 0.4 convolution_add_fusion.13
  49.7 6.7 %all_to_all.8 = bf16[96,4,2,48]{0,3,2,1:T(8,128)(2,1)S(1)} all-to-all(bf16[96,4,2,48]{0,3,2,1:T(8,128)(2,1)S(1)} %bitcast.270), channel_id=1, replica_groups=mesh['clips'=2,'tm'=4,'rows'=4] {'tm'}, dimensions={1} | all-to-all | bytes 147456 | tf_op jit(solution)/shard_map/all_to_all | solution.py:66
  56.9 10.1 %psum.44 = f32[1,32]{1,0:T(1,128)S(1)} all-reduce(f32[1,32]{1,0:T(1,128)S(1)} %bitcast.279), channel_id=1, replica_groups=mesh['clips'=2,'tm'=4,'rows'=4] {'rows'}, use_global_device_ids=true, to_apply=%region_8.9 | all-reduce | flops 32 | bytes 256 | tf_op jit(solution)/shard_map/psum | solution.py:32
  67.5 8.7 %psum.45 = f32[1,32]{1,0:T(1,128)S(1)} all-reduce(f32[1,32]{1,0:T(1,128)S(1)} %bitcast.280), channel_id=1, replica_groups=mesh['clips'=2,'tm'=4,'rows'=4] {'rows'}, use_global_device_ids=true, to_apply=%region_11.12 | all-reduce | flops 32 | bytes 256 | tf_op jit(solution)/shard_map/psum | solution.py:35
  76.4 3.6 %collective-permute-start.2 = (bf16[1,1,48,384]{3,2,1,0:T(8,128)(2,1)S(1)}, bf16[1,1,48,384]{3,2,1,0:T(8,128)(2,1)S(1)}, u32[]{:S(2)}, u32[]{:S(2)}) collective-permute-start(bf16[1,1,48,384]{3,2,1,0:T(8,128)(2,1)S(1)} %get-tuple-element.79), channel_id=1, source_target_pairs={{0,1},{1,2},{2,3},{4,5},{5,6},{6,7},{8,9},{9,10},{10,11},{12,13},{... | collective-permute-start | bytes 110600 | tf_op jit(solution)/shard_map/ppermute | solution.py:19
  80.0 1.3 collective-permute-start.3
  83.3 2.5 %collective-permute-done.3 = bf16[1,1,48,384]{3,2,1,0:T(8,128)(2,1)S(1)} collective-permute-done((bf16[1,1,48,384]{3,2,1,0:T(8,128)(2,1)S(1)}, bf16[1,1,48,384]{3,2,1,0:T(8,128)(2,1)S(1)}, u32[]{:S(2)}, u32[]{:S(2)}) %collective-permute-start.3) | collective-permute-done | bytes 36896 | tf_op jit(solution)/shard_map/ppermute | solution.py:21
  85.9 6.9 %all_gather.13 = bf16[4,4,48,384]{3,2,1,0:T(8,128)(2,1)S(1)} all-gather(bf16[1,4,48,384]{3,2,1,0:T(8,128)(2,1)S(1)} %pad_maximum_fusion.19), channel_id=1, replica_groups=mesh['clips'=2,'tm'=4,'rows'=4] {'tm'}, dimensions={0}, use_global_device_ids=true | all-gather | bytes 737280 | tf_op jit(solution)/shard_map/all_gather | solution.py:42
  92.8 1.7 %pad_slice_fusion.1 = (bf16[4,2,48,384]{3,2,1,0:T(8,128)(2,1)S(1)}, bf16[4,2,48,384]{3,2,1,0:T(8,128)(2,1)S(1)}, bf16[4,2,48,384]{3,2,1,0:T(8,128)(2,1)S(1)}, bf...) fusion(bf16[4,4,48,384]{3,2,1,0:T(8,128)(2,1)S(1)} %all_gather.13), kind=kLoop, calls=%fused_computation.1 | loop fusion | bytes 6193152 | tf_op jit(solution)/shard_map/slice | solution.py:52
  97.7 0.4 convolution_add_fusion.4
  98.5 0.4 convolution_add_fusion.2
  99.0 0.4 fusion.11
  99.5 6.7 %all_to_all.9 = bf16[96,4,2,48]{0,3,2,1:T(8,128)(2,1)S(1)} all-to-all(bf16[96,4,2,48]{0,3,2,1:T(8,128)(2,1)S(1)} %bitcast.271), channel_id=1, replica_groups=mesh['clips'=2,'tm'=4,'rows'=4] {'tm'}, dimensions={1} | all-to-all | bytes 147456 | tf_op jit(solution)/shard_map/all_to_all | solution.py:66
  106.8 8.5 %psum.46 = f32[1,32]{1,0:T(1,128)S(1)} all-reduce(f32[1,32]{1,0:T(1,128)S(1)} %bitcast.281), channel_id=1, replica_groups=mesh['clips'=2,'tm'=4,'rows'=4] {'rows'}, use_global_device_ids=true, to_apply=%region_14.15 | all-reduce | flops 32 | bytes 256 | tf_op jit(solution)/shard_map/psum | solution.py:32
  115.8 10.2 %psum.47 = f32[1,32]{1,0:T(1,128)S(1)} all-reduce(f32[1,32]{1,0:T(1,128)S(1)} %bitcast.276), channel_id=1, replica_groups=mesh['clips'=2,'tm'=4,'rows'=4] {'rows'}, use_global_device_ids=true, to_apply=%region_17.18 | all-reduce | flops 32 | bytes 256 | tf_op jit(solution)/shard_map/psum | solution.py:35
  126.5 14.7 %all_gather.14 = bf16[1,8,48,384]{3,2,0,1:T(8,128)(2,1)S(1)} all-gather(bf16[1,2,48,384]{3,2,0,1:T(8,128)(2,1)S(1)} %bitcast.274), channel_id=1, replica_groups=mesh['clips'=2,'tm'=4,'rows'=4] {'rows'}, dimensions={1}, use_global_device_ids=true | all-gather | bytes 368640 | tf_op jit(solution)/shard_map/all_gather | solution.py:131
  141.2 0.5 fusion.50
  142.1 14.1 %all_gather.15 = bf16[1,8,48,384]{3,2,0,1:T(8,128)(2,1)S(1)} all-gather(bf16[1,2,48,384]{3,2,0,1:T(8,128)(2,1)S(1)} %bitcast.273), channel_id=1, replica_groups=mesh['clips'=2,'tm'=4,'rows'=4] {'rows'}, dimensions={1}, use_global_device_ids=true | all-gather | bytes 368640 | tf_op jit(solution)/shard_map/all_gather | solution.py:134
  156.4 0.8 fusion.4
  (144 shorter events, 15.0 us)
Async XLA Ops:
  0.0 141.2 %copy-start = (bf16[384,384]{1,0:T(8,128)(2,1)S(1)}, bf16[384,384]{1,0:T(8,128)(2,1)}, u32[]{:S(2)}) copy-start(bf16[384,384]{1,0:T(8,128)(2,1)} %param.26) | copy-start | bytes 884740
  25.5 8.8 %collective-permute-start = (bf16[1,1,48,384]{3,2,1,0:T(8,128)(2,1)S(1)}, bf16[1,1,48,384]{3,2,1,0:T(8,128)(2,1)S(1)}, u32[]{:S(2)}, u32[]{:S(2)}) collective-permute-start(bf16[1,1,48,384]{3,2,1,0:T(8,128)(2,1)S(1)} %get-tuple-element.81), channel_id=1, source_target_pairs={{0,1},{1,2},{2,3},{4,5},{5,6},{6,7},{8,9},{9,10},{10,11},{12,13},{... | collective-permute-start | bytes 110600 | tf_op jit(solution)/shard_map/ppermute | solution.py:19
  29.4 5.9 %collective-permute-start.1 = (bf16[1,1,48,384]{3,2,1,0:T(8,128)(2,1)S(1)}, bf16[1,1,48,384]{3,2,1,0:T(8,128)(2,1)S(1)}, u32[]{:S(2)}, u32[]{:S(2)}) collective-permute-start(bf16[1,1,48,384]{3,2,1,0:T(8,128)(2,1)S(1)} %get-tuple-element.82), channel_id=1, source_target_pairs={{1,0},{2,1},{3,2},{5,4},{6,5},{7,6},{9,8},{10,9},{11,10},{13,12},{... | collective-permute-start | bytes 110600 | tf_op jit(solution)/shard_map/ppermute | solution.py:21
  48.5 0.7 copy-start.10
  49.0 27.3 %copy-start.6 = (f32[384]{0:T(512)S(1)}, f32[384]{0:T(512)}, u32[]{:S(2)}) copy-start(f32[384]{0:T(512)} %param.21) | copy-start | bytes 4612
  49.0 27.3 %copy-start.7 = (f32[384]{0:T(512)S(1)}, f32[384]{0:T(512)}, u32[]{:S(2)}) copy-start(f32[384]{0:T(512)} %param.20) | copy-start | bytes 4612
  49.0 32.3 %copy-start.1 = (bf16[96,3,3,3,384]{4,0,3,2,1:T(8,128)(2,1)S(1)}, bf16[96,3,3,3,384]{4,0,3,2,1:T(8,128)(2,1)}, u32[]{:S(2)}) copy-start(bf16[96,3,3,3,384]{4,0,3,2,1:T(8,128)(2,1)} %param.22) | copy-start | bytes 5971972
  76.4 6.9 %collective-permute-start.2 = (bf16[1,1,48,384]{3,2,1,0:T(8,128)(2,1)S(1)}, bf16[1,1,48,384]{3,2,1,0:T(8,128)(2,1)S(1)}, u32[]{:S(2)}, u32[]{:S(2)}) collective-permute-start(bf16[1,1,48,384]{3,2,1,0:T(8,128)(2,1)S(1)} %get-tuple-element.79), channel_id=1, source_target_pairs={{0,1},{1,2},{2,3},{4,5},{5,6},{6,7},{8,9},{9,10},{10,11},{12,13},{... | collective-permute-start | bytes 110600 | tf_op jit(solution)/shard_map/ppermute | solution.py:19
  80.0 5.9 %collective-permute-start.3 = (bf16[1,1,48,384]{3,2,1,0:T(8,128)(2,1)S(1)}, bf16[1,1,48,384]{3,2,1,0:T(8,128)(2,1)S(1)}, u32[]{:S(2)}, u32[]{:S(2)}) collective-permute-start(bf16[1,1,48,384]{3,2,1,0:T(8,128)(2,1)S(1)} %get-tuple-element.80), channel_id=1, source_target_pairs={{1,0},{2,1},{3,2},{5,4},{6,5},{7,6},{9,8},{10,9},{11,10},{13,12},{... | collective-permute-start | bytes 110600 | tf_op jit(solution)/shard_map/ppermute | solution.py:21
  97.7 1.3 copy-start.11
  98.5 8.1 %copy-start.2 = (bf16[1,2,48,384]{3,2,1,0:T(8,128)(2,1)S(1)}, bf16[1,2,48,384]{3,2,1,0:T(8,128)(2,1)}, u32[]{:S(2)}) copy-start(bf16[1,2,48,384]{3,2,1,0:T(8,128)(2,1)} %param.15) | copy-start | bytes 221188
  98.9 27.3 %copy-start.8 = (f32[384]{0:T(512)S(1)}, f32[384]{0:T(512)}, u32[]{:S(2)}) copy-start(f32[384]{0:T(512)} %param.25) | copy-start | bytes 4612
  99.0 27.3 %copy-start.9 = (f32[384]{0:T(512)S(1)}, f32[384]{0:T(512)}, u32[]{:S(2)}) copy-start(f32[384]{0:T(512)} %param.24) | copy-start | bytes 4612
  99.0 27.4 %copy-start.3 = (bf16[384,384]{1,0:T(8,128)(2,1)S(1)}, bf16[384,384]{1,0:T(8,128)(2,1)}, u32[]{:S(2)}) copy-start(bf16[384,384]{1,0:T(8,128)(2,1)} %param.27) | copy-start | bytes 884740
  106.3 35.6 %copy-start.4 = (bf16[384,384]{1,0:T(8,128)(2,1)S(1)}, bf16[384,384]{1,0:T(8,128)(2,1)}, u32[]{:S(2)}) copy-start(bf16[384,384]{1,0:T(8,128)(2,1)} %param.28) | copy-start | bytes 884740
  126.3 30.1 %copy-start.5 = (bf16[384,384]{1,0:T(8,128)(2,1)S(1)}, bf16[384,384]{1,0:T(8,128)(2,1)}, u32[]{:S(2)}) copy-start(bf16[384,384]{1,0:T(8,128)(2,1)} %param.29) | copy-start | bytes 884740
where the time goes:
time: 158 us; the launch traced here: 157 us
  blocking collectives  116 us (73%)
  local copies, waits for them, and re-layouts  12.1 us (8%)
  starting transfers between devices  10.1 us (6%)
  matrix products  9.27 us (6%)
  other arithmetic  5.53 us (4%)
  waiting for transfers between devices  3.52 us (2%)
    psum x3, blocking collectives, group_norm(): sums = lax.psum(jnp.sum(grouped, axis=(1, 2, 4)), 'rows')  32.1 us
    psum x3, blocking collectives, group_norm(): lax.psum(jnp.sum(centered * centered, axis=(1, 2, 4)), 'rows') / entries  27.3 us
    all_gather x1, blocking collectives, per_device(): lax.all_gather(keys.reshape(shape4), 'rows', axis=1, tiled=True)  14.7 us
    all_gather x2, blocking collectives, causal_conv(): clip_frames = lax.all_gather(widened, 'tm', axis=0, tiled=True)  14.4 us
    all_gather x1, blocking collectives, per_device(): lax.all_gather(values.reshape(shape4), 'rows', axis=1, tiled=True)  14.1 us
    all_to_all x2, blocking collectives, causal_conv(): lax.all_to_all(result, 'tm', split_axis=1, concat_axis=0, tiled=True)  13.4 us
    ppermute x2, starting transfers between devices, extended(): lax.ppermute(tail, axis, [(i, (i + 1) % count) for i in range(ends)])  7.47 us
    dot_general x18, matrix products, causal_conv(): lax.dot_general(tap_weight, stacked.reshape(-1, 3 * channels), (((1,), (1...  7.32 us
  transfers between devices with their start and end apart: 4, of which 2 were waited for; matrix products, arithmetic and copies ran while one was open for 3% of the time, Pallas kernels for 0%

commit v1 on v0

--- a/solution.py
+++ b/solution.py
@@ -63,7 +63,19 @@
         .astype(jnp.bfloat16)
         .reshape(outputs, frame_count, row_count, col_count)
     )
-    mixed = lax.all_to_all(result, "tm", split_axis=1, concat_axis=0, tiled=True)
+    ways, here = (lax.axis_size("tm"), lax.axis_index("tm"))
+    width_2 = result.shape[1] // ways
+    lengths = list(result.shape)
+    lengths[1] = width_2
+    height = lengths[0]
+    lengths[0] = height * ways
+    full = jnp.zeros(lengths, result.dtype)
+    for mask in range(ways):
+        part = lax.dynamic_slice_in_dim(result, (here ^ mask) * width_2, width_2, axis=1)
+        if mask:
+            part = lax.ppermute(part, "tm", [(d, d ^ mask) for d in range(ways)])
+        full = lax.dynamic_update_slice_in_dim(full, part, (here ^ mask) * height, axis=0)
+    mixed = full
     return jnp.transpose(mixed, (1, 2, 3, 0))
 
 

time: 158 us -> 155 us (0.981)
  blocking collectives: 116 us -> 102 us
  starting transfers between devices: 10.1 us -> 14 us
  waiting for transfers between devices: 3.52 us -> 6.85 us
  local copies, waits for them, and re-layouts: 12.1 us -> 15.2 us
    all_to_all x2 -> x0, blocking collectives: 13.4 us -> none  [causal_conv(): lax.all_to_all(result, 'tm', split_axis=1, concat_axis=0, tiled=True)]
    ppermute x0 -> x6, starting transfers between devices: none -> 3.85 us  [causal_conv(): part = lax.ppermute(part, 'tm', [(d, d ^ mask) for d in range(ways)])]
    dynamic_update_slice x0 -> x8, local copies, waits for them, and re-layouts: none -> 3.5 us  [causal_conv(): lax.dynamic_update_slice_in_dim(full, part, (here ^ mask) * height, axis=0)]
    ppermute x0 -> x6, waiting for transfers between devices: none -> 3.4 us  [causal_conv(): part = lax.ppermute(part, 'tm', [(d, d ^ mask) for d in range(ways)])]
  transfers between devices with their start and end apart: 4 -> 10, of which waited for: 2 -> 5; matrix products, arithmetic and copies ran while one was open for 3% -> 5% of each run, Pallas kernels for 0% -> 0%
where the time goes in v1:
time: 155 us; the launch traced here: 154 us
  blocking collectives  102 us (66%)
  local copies, waits for them, and re-layouts  15.2 us (10%)
  starting transfers between devices  14 us (9%)
  matrix products  9.27 us (6%)
  waiting for transfers between devices  6.85 us (4%)
  other arithmetic  5.51 us (4%)
    psum x3, blocking collectives, group_norm(): sums = lax.psum(jnp.sum(grouped, axis=(1, 2, 4)), 'rows')  32.2 us
    psum x3, blocking collectives, group_norm(): lax.psum(jnp.sum(centered * centered, axis=(1, 2, 4)), 'rows') / entries  27.4 us
    all_gather x2, blocking collectives, causal_conv(): clip_frames = lax.all_gather(widened, 'tm', axis=0, tiled=True)  14.7 us
    all_gather x1, blocking collectives, per_device(): lax.all_gather(keys.reshape(shape4), 'rows', axis=1, tiled=True)  14.1 us
    all_gather x1, blocking collectives, per_device(): lax.all_gather(values.reshape(shape4), 'rows', axis=1, tiled=True)  13.9 us
    ppermute x2, starting transfers between devices, extended(): lax.ppermute(tail, axis, [(i, (i + 1) % count) for i in range(ends)])  7.55 us
    dot_general x18, matrix products, causal_conv(): lax.dot_general(tap_weight, stacked.reshape(-1, 3 * channels), (((1,), (1...  7.33 us
    slice x20, local copies, waits for them, and re-layouts, causal_conv(): tap_weight = kernel[:, tap_time, tap_row].reshape(outputs, 3 * channels)  4.82 us
  transfers between devices with their start and end apart: 10, of which 5 were waited for; matrix products, arithmetic and copies ran while one was open for 5% of the time, Pallas kernels for 0%

profile of v1, /device:TPU:0, one launch (start us, length us, event | category | flops | bytes accessed | tf_op | source)
XLA Modules:
  0.0 154.1 jit_solution(6354996630325969175)
XLA Ops:
  0.0 1.0 convert_reduce_fusion.1
  1.2 13.5 %psum.42 = f32[1,32]{1,0:T(1,128)S(1)} all-reduce(f32[1,32]{1,0:T(1,128)S(1)} %bitcast.262), channel_id=1, replica_groups=mesh['clips'=2,'tm'=4,'rows'=4] {'rows'}, use_global_device_ids=true, to_apply=%region_2.0 | all-reduce | flops 32 | bytes 256 | tf_op jit(solution)/shard_map/psum | solution.py:32
  14.8 0.9 fusion.23
  16.0 8.4 %psum.43 = f32[1,32]{1,0:T(1,128)S(1)} all-reduce(f32[1,32]{1,0:T(1,128)S(1)} %bitcast.263), channel_id=1, replica_groups=mesh['clips'=2,'tm'=4,'rows'=4] {'rows'}, use_global_device_ids=true, to_apply=%region_5.6 | all-reduce | flops 32 | bytes 256 | tf_op jit(solution)/shard_map/psum | solution.py:35
  24.5 1.0 fusion.31
  25.5 3.9 %collective-permute-start = (bf16[1,1,48,384]{3,2,1,0:T(8,128)(2,1)S(1)}, bf16[1,1,48,384]{3,2,1,0:T(8,128)(2,1)S(1)}, u32[]{:S(2)}, u32[]{:S(2)}) collective-permute-start(bf16[1,1,48,384]{3,2,1,0:T(8,128)(2,1)S(1)} %get-tuple-element.89), channel_id=1, source_target_pairs={{0,1},{1,2},{2,3},{4,5},{5,6},{6,7},{8,9},{9,10},{10,11},{12,13},{... | collective-permute-start | bytes 110600 | tf_op jit(solution)/shard_map/ppermute | solution.py:19
  29.4 1.3 collective-permute-start.1
  30.7 1.8 %fusion.52 = (bf16[96,1,1,3,384]{4,0,3,2,1:T(8,128)(2,1)S(1)}, bf16[96,1,1,3,384]{4,0,3,2,1:T(8,128)(2,1)S(1)}, bf16[96,1,1,3,384]{4,0,3,2,1:T(8,128)(2,1)S(1)},...) fusion(bf16[96,3,3,3,384]{4,0,3,2,1:T(8,128)(2,1)} %param.18), kind=kLoop, calls=%fused_computation.162 | loop fusion | bytes 3981312 | tf_op jit(solution)/shard_map/slice | solution.py:54
  34.4 0.9 collective-permute-done.1
  35.3 7.5 %all_gather.12 = bf16[4,4,48,384]{3,2,1,0:T(8,128)(2,1)S(1)} all-gather(bf16[1,4,48,384]{3,2,1,0:T(8,128)(2,1)S(1)} %pad_maximum_fusion.18), channel_id=1, replica_groups=mesh['clips'=2,'tm'=4,'rows'=4] {'tm'}, dimensions={0}, use_global_device_ids=true | all-gather | bytes 737280 | tf_op jit(solution)/shard_map/all_gather | solution.py:42
  42.8 1.8 %pad_slice_fusion.25 = (bf16[4,2,48,384]{3,2,1,0:T(8,128)(2,1)S(1)}, bf16[4,2,48,384]{3,2,1,0:T(8,128)(2,1)S(1)}, bf16[4,2,48,384]{3,2,1,0:T(8,128)(2,1)S(1)}, b...) fusion(bf16[4,4,48,384]{3,2,1,0:T(8,128)(2,1)S(1)} %all_gather.12), kind=kLoop, calls=%fused_computation.25 | loop fusion | bytes 6193152 | tf_op jit(solution)/shard_map/slice | solution.py:52
  50.2 0.7 collective-permute-start.3
  50.8 0.8 collective-permute-start.4
  51.9 0.5 dynamic_update_slice.25
  52.5 1.7 %collective-permute-done.3 = bf16[96,1,2,48]{0,3,2,1:T(8,128)(2,1)S(1)} collective-permute-done((bf16[96,1,2,48]{0,3,2,1:T(8,128)(2,1)S(1)}, bf16[96,1,2,48]{0,3,2,1:T(8,128)(2,1)S(1)}, u32[]{:S(2)}, u32[]{:S(2)}) %collective-permute-start.3) | collective-permute-done | bytes 18464 | tf_op jit(solution)/shard_map/ppermute | solution.py:76
  54.2 0.5 dynamic_update_slice.26
  54.7 0.5 dynamic_update_slice.27
  55.4 10.2 %psum.44 = f32[1,32]{1,0:T(1,128)S(1)} all-reduce(f32[1,32]{1,0:T(1,128)S(1)} %bitcast.264), channel_id=1, replica_groups=mesh['clips'=2,'tm'=4,'rows'=4] {'rows'}, use_global_device_ids=true, to_apply=%region_8.9 | all-reduce | flops 32 | bytes 256 | tf_op jit(solution)/shard_map/psum | solution.py:32
  66.1 8.6 %psum.45 = f32[1,32]{1,0:T(1,128)S(1)} all-reduce(f32[1,32]{1,0:T(1,128)S(1)} %bitcast.265), channel_id=1, replica_groups=mesh['clips'=2,'tm'=4,'rows'=4] {'rows'}, use_global_device_ids=true, to_apply=%region_11.12 | all-reduce | flops 32 | bytes 256 | tf_op jit(solution)/shard_map/psum | solution.py:35
  75.0 3.7 %collective-permute-start.5 = (bf16[1,1,48,384]{3,2,1,0:T(8,128)(2,1)S(1)}, bf16[1,1,48,384]{3,2,1,0:T(8,128)(2,1)S(1)}, u32[]{:S(2)}, u32[]{:S(2)}) collective-permute-start(bf16[1,1,48,384]{3,2,1,0:T(8,128)(2,1)S(1)} %get-tuple-element.87), channel_id=1, source_target_pairs={{0,1},{1,2},{2,3},{4,5},{5,6},{6,7},{8,9},{9,10},{10,11},{12,13},{... | collective-permute-start | bytes 110600 | tf_op jit(solution)/shard_map/ppermute | solution.py:19
  78.6 1.3 collective-permute-start.6
  81.9 2.5 %collective-permute-done.6 = bf16[1,1,48,384]{3,2,1,0:T(8,128)(2,1)S(1)} collective-permute-done((bf16[1,1,48,384]{3,2,1,0:T(8,128)(2,1)S(1)}, bf16[1,1,48,384]{3,2,1,0:T(8,128)(2,1)S(1)}, u32[]{:S(2)}, u32[]{:S(2)}) %collective-permute-start.6) | collective-permute-done | bytes 36896 | tf_op jit(solution)/shard_map/ppermute | solution.py:21
  84.5 7.2 %all_gather.13 = bf16[4,4,48,384]{3,2,1,0:T(8,128)(2,1)S(1)} all-gather(bf16[1,4,48,384]{3,2,1,0:T(8,128)(2,1)S(1)} %pad_maximum_fusion.19), channel_id=1, replica_groups=mesh['clips'=2,'tm'=4,'rows'=4] {'tm'}, dimensions={0}, use_global_device_ids=true | all-gather | bytes 737280 | tf_op jit(solution)/shard_map/all_gather | solution.py:42
  91.7 1.7 %pad_slice_fusion.1 = (bf16[4,2,48,384]{3,2,1,0:T(8,128)(2,1)S(1)}, bf16[4,2,48,384]{3,2,1,0:T(8,128)(2,1)S(1)}, bf16[4,2,48,384]{3,2,1,0:T(8,128)(2,1)S(1)}, bf...) fusion(bf16[4,4,48,384]{3,2,1,0:T(8,128)(2,1)S(1)} %all_gather.13), kind=kLoop, calls=%fused_computation.1 | loop fusion | bytes 6193152 | tf_op jit(solution)/shard_map/slice | solution.py:52
  98.9 1.1 collective-permute-start.8
  100.7 0.5 dynamic_update_slice.29
  101.2 1.5 collective-permute-done.8
  104.2 8.5 %psum.46 = f32[1,32]{1,0:T(1,128)S(1)} all-reduce(f32[1,32]{1,0:T(1,128)S(1)} %bitcast.266), channel_id=1, replica_groups=mesh['clips'=2,'tm'=4,'rows'=4] {'rows'}, use_global_device_ids=true, to_apply=%region_14.15 | all-reduce | flops 32 | bytes 256 | tf_op jit(solution)/shard_map/psum | solution.py:32
  113.2 10.5 %psum.47 = f32[1,32]{1,0:T(1,128)S(1)} all-reduce(f32[1,32]{1,0:T(1,128)S(1)} %bitcast.261), channel_id=1, replica_groups=mesh['clips'=2,'tm'=4,'rows'=4] {'rows'}, use_global_device_ids=true, to_apply=%region_17.18 | all-reduce | flops 32 | bytes 256 | tf_op jit(solution)/shard_map/psum | solution.py:35
  124.1 14.1 %all_gather.14 = bf16[1,8,48,384]{3,2,0,1:T(8,128)(2,1)S(1)} all-gather(bf16[1,2,48,384]{3,2,0,1:T(8,128)(2,1)S(1)} %bitcast.259), channel_id=1, replica_groups=mesh['clips'=2,'tm'=4,'rows'=4] {'rows'}, dimensions={1}, use_global_device_ids=true | all-gather | bytes 368640 | tf_op jit(solution)/shard_map/all_gather | solution.py:143
  139.1 13.9 %all_gather.15 = bf16[1,8,48,384]{3,2,0,1:T(8,128)(2,1)S(1)} all-gather(bf16[1,2,48,384]{3,2,0,1:T(8,128)(2,1)S(1)} %bitcast.258), channel_id=1, replica_groups=mesh['clips'=2,'tm'=4,'rows'=4] {'rows'}, dimensions={1}, use_global_device_ids=true | all-gather | bytes 368640 | tf_op jit(solution)/shard_map/all_gather | solution.py:146
  153.2 0.8 fusion.4
  (160 shorter events, 20.3 us)
Async XLA Ops:
  0.0 138.2 %copy-start = (bf16[384,384]{1,0:T(8,128)(2,1)S(1)}, bf16[384,384]{1,0:T(8,128)(2,1)}, u32[]{:S(2)}) copy-start(bf16[384,384]{1,0:T(8,128)(2,1)} %param.26) | copy-start | bytes 884740
  25.5 8.8 %collective-permute-start = (bf16[1,1,48,384]{3,2,1,0:T(8,128)(2,1)S(1)}, bf16[1,1,48,384]{3,2,1,0:T(8,128)(2,1)S(1)}, u32[]{:S(2)}, u32[]{:S(2)}) collective-permute-start(bf16[1,1,48,384]{3,2,1,0:T(8,128)(2,1)S(1)} %get-tuple-element.89), channel_id=1, source_target_pairs={{0,1},{1,2},{2,3},{4,5},{5,6},{6,7},{8,9},{9,10},{10,11},{12,13},{... | collective-permute-start | bytes 110600 | tf_op jit(solution)/shard_map/ppermute | solution.py:19
  29.4 5.9 %collective-permute-start.1 = (bf16[1,1,48,384]{3,2,1,0:T(8,128)(2,1)S(1)}, bf16[1,1,48,384]{3,2,1,0:T(8,128)(2,1)S(1)}, u32[]{:S(2)}, u32[]{:S(2)}) collective-permute-start(bf16[1,1,48,384]{3,2,1,0:T(8,128)(2,1)S(1)} %get-tuple-element.90), channel_id=1, source_target_pairs={{1,0},{2,1},{3,2},{5,4},{6,5},{7,6},{9,8},{10,9},{11,10},{13,12},{... | collective-permute-start | bytes 110600 | tf_op jit(solution)/shard_map/ppermute | solution.py:21
  48.5 0.7 copy-start.10
  48.6 26.2 %copy-start.6 = (f32[384]{0:T(512)S(1)}, f32[384]{0:T(512)}, u32[]{:S(2)}) copy-start(f32[384]{0:T(512)} %param.21) | copy-start | bytes 4612
  48.6 26.2 %copy-start.7 = (f32[384]{0:T(512)S(1)}, f32[384]{0:T(512)}, u32[]{:S(2)}) copy-start(f32[384]{0:T(512)} %param.20) | copy-start | bytes 4612
  48.6 31.3 %copy-start.1 = (bf16[96,3,3,3,384]{4,0,3,2,1:T(8,128)(2,1)S(1)}, bf16[96,3,3,3,384]{4,0,3,2,1:T(8,128)(2,1)}, u32[]{:S(2)}) copy-start(bf16[96,3,3,3,384]{4,0,3,2,1:T(8,128)(2,1)} %param.22) | copy-start | bytes 5971972
  49.7 2.2 %collective-permute-start.2 = (bf16[96,1,2,48]{0,3,2,1:T(8,128)(2,1)S(1)}, bf16[96,1,2,48]{0,3,2,1:T(8,128)(2,1)S(1)}, u32[]{:S(2)}, u32[]{:S(2)}) collective-permute-start(bf16[96,1,2,48]{0,3,2,1:T(8,128)(2,1)S(1)} %get-tuple-element.85), channel_id=1, source_target_pairs={{0,4},{4,0},{8,12},{12,8},{1,5},{5,1},{9,13},{13,9},{2,6},{6,2},{1... | collective-permute-start | bytes 55304 | tf_op jit(solution)/shard_map/ppermute | solution.py:76
  50.2 4.0 %collective-permute-start.3 = (bf16[96,1,2,48]{0,3,2,1:T(8,128)(2,1)S(1)}, bf16[96,1,2,48]{0,3,2,1:T(8,128)(2,1)S(1)}, u32[]{:S(2)}, u32[]{:S(2)}) collective-permute-start(bf16[96,1,2,48]{0,3,2,1:T(8,128)(2,1)S(1)} %get-tuple-element.84), channel_id=1, source_target_pairs={{0,8},{4,12},{8,0},{12,4},{1,9},{5,13},{9,1},{13,5},{2,10},{6,14},... | collective-permute-start | bytes 55304 | tf_op jit(solution)/shard_map/ppermute | solution.py:76
  50.8 3.9 %collective-permute-start.4 = (bf16[96,1,2,48]{0,3,2,1:T(8,128)(2,1)S(1)}, bf16[96,1,2,48]{0,3,2,1:T(8,128)(2,1)S(1)}, u32[]{:S(2)}, u32[]{:S(2)}) collective-permute-start(bf16[96,1,2,48]{0,3,2,1:T(8,128)(2,1)S(1)} %get-tuple-element.83), channel_id=1, source_target_pairs={{0,12},{4,8},{8,4},{12,0},{1,13},{5,9},{9,5},{13,1},{2,14},{6,10},... | collective-permute-start | bytes 55304 | tf_op jit(solution)/shard_map/ppermute | solution.py:76
  75.0 7.0 %collective-permute-start.5 = (bf16[1,1,48,384]{3,2,1,0:T(8,128)(2,1)S(1)}, bf16[1,1,48,384]{3,2,1,0:T(8,128)(2,1)S(1)}, u32[]{:S(2)}, u32[]{:S(2)}) collective-permute-start(bf16[1,1,48,384]{3,2,1,0:T(8,128)(2,1)S(1)} %get-tuple-element.87), channel_id=1, source_target_pairs={{0,1},{1,2},{2,3},{4,5},{5,6},{6,7},{8,9},{9,10},{10,11},{12,13},{... | collective-permute-start | bytes 110600 | tf_op jit(solution)/shard_map/ppermute | solution.py:19
  78.6 5.9 %collective-permute-start.6 = (bf16[1,1,48,384]{3,2,1,0:T(8,128)(2,1)S(1)}, bf16[1,1,48,384]{3,2,1,0:T(8,128)(2,1)S(1)}, u32[]{:S(2)}, u32[]{:S(2)}) collective-permute-start(bf16[1,1,48,384]{3,2,1,0:T(8,128)(2,1)S(1)} %get-tuple-element.88), channel_id=1, source_target_pairs={{1,0},{2,1},{3,2},{5,4},{6,5},{7,6},{9,8},{10,9},{11,10},{13,12},{... | collective-permute-start | bytes 110600 | tf_op jit(solution)/shard_map/ppermute | solution.py:21
  96.6 1.3 copy-start.11
  97.4 6.5 %copy-start.2 = (bf16[1,2,48,384]{3,2,1,0:T(8,128)(2,1)S(1)}, bf16[1,2,48,384]{3,2,1,0:T(8,128)(2,1)}, u32[]{:S(2)}) copy-start(bf16[1,2,48,384]{3,2,1,0:T(8,128)(2,1)} %param.15) | copy-start | bytes 221188
  97.4 26.4 %copy-start.8 = (f32[384]{0:T(512)S(1)}, f32[384]{0:T(512)}, u32[]{:S(2)}) copy-start(f32[384]{0:T(512)} %param.25) | copy-start | bytes 4612
  97.5 26.4 %copy-start.9 = (f32[384]{0:T(512)S(1)}, f32[384]{0:T(512)}, u32[]{:S(2)}) copy-start(f32[384]{0:T(512)} %param.24) | copy-start | bytes 4612
  97.5 26.4 %copy-start.3 = (bf16[384,384]{1,0:T(8,128)(2,1)S(1)}, bf16[384,384]{1,0:T(8,128)(2,1)}, u32[]{:S(2)}) copy-start(bf16[384,384]{1,0:T(8,128)(2,1)} %param.27) | copy-start | bytes 884740
  98.3 40.5 %copy-start.4 = (bf16[384,384]{1,0:T(8,128)(2,1)S(1)}, bf16[384,384]{1,0:T(8,128)(2,1)}, u32[]{:S(2)}) copy-start(bf16[384,384]{1,0:T(8,128)(2,1)} %param.28) | copy-start | bytes 884740
  98.5 2.2 %collective-permute-start.7 = (bf16[96,1,2,48]{0,3,2,1:T(8,128)(2,1)S(1)}, bf16[96,1,2,48]{0,3,2,1:T(8,128)(2,1)S(1)}, u32[]{:S(2)}, u32[]{:S(2)}) collective-permute-start(bf16[96,1,2,48]{0,3,2,1:T(8,128)(2,1)S(1)} %get-tuple-element.81), channel_id=1, source_target_pairs={{0,4},{4,0},{8,12},{12,8},{1,5},{5,1},{9,13},{13,9},{2,6},{6,2},{1... | collective-permute-start | bytes 55304 | tf_op jit(solution)/shard_map/ppermute | solution.py:76
  98.9 3.8 %collective-permute-start.8 = (bf16[96,1,2,48]{0,3,2,1:T(8,128)(2,1)S(1)}, bf16[96,1,2,48]{0,3,2,1:T(8,128)(2,1)S(1)}, u32[]{:S(2)}, u32[]{:S(2)}) collective-permute-start(bf16[96,1,2,48]{0,3,2,1:T(8,128)(2,1)S(1)} %get-tuple-element.80), channel_id=1, source_target_pairs={{0,8},{4,12},{8,0},{12,4},{1,9},{5,13},{9,1},{13,5},{2,10},{6,14},... | collective-permute-start | bytes 55304 | tf_op jit(solution)/shard_map/ppermute | solution.py:76
  100.0 3.5 %collective-permute-start.9 = (bf16[96,1,2,48]{0,3,2,1:T(8,128)(2,1)S(1)}, bf16[96,1,2,48]{0,3,2,1:T(8,128)(2,1)S(1)}, u32[]{:S(2)}, u32[]{:S(2)}) collective-permute-start(bf16[96,1,2,48]{0,3,2,1:T(8,128)(2,1)S(1)} %get-tuple-element.79), channel_id=1, source_target_pairs={{0,12},{4,8},{8,4},{12,0},{1,13},{5,9},{9,5},{13,1},{2,14},{6,10},... | collective-permute-start | bytes 55304 | tf_op jit(solution)/shard_map/ppermute | solution.py:76
  123.9 29.3 %copy-start.5 = (bf16[384,384]{1,0:T(8,128)(2,1)S(1)}, bf16[384,384]{1,0:T(8,128)(2,1)}, u32[]{:S(2)}) copy-start(bf16[384,384]{1,0:T(8,128)(2,1)} %param.29) | copy-start | bytes 884740
